TPU v7x, 256 devices: a whole 4x4x8 slice. The times are simulated.
256 devices in a mesh: ctx: 16 (over y_lo, z), head: 16 (over x, y_hi, core).
Axes of the slice: x: 4, y: 4 (y_hi: 2, y_lo: 2; y = y_hi * 2 + y_lo), z: 8, core: 2. Of those that a mesh axis runs over, the one named last changes fastest.
Arguments:
- q_noisy: bfloat16 [8192, 2048], P('ctx', 'head'), may hold values from -8 to 8
- k_noisy: bfloat16 [8192, 2048], P('ctx', 'head'), may hold values from -8 to 8
- v_noisy: bfloat16 [8192, 2048], P('ctx', 'head'), may hold values from -8 to 8
- k_clean: bfloat16 [8192, 2048], P('ctx', 'head'), may hold values from -8 to 8
- v_clean: bfloat16 [8192, 2048], P('ctx', 'head'), may hold values from -8 to 8
- out_weight: bfloat16 [2048, 4096], P('head'), may hold values from -0.1875 to 0.1875
- cotangent: bfloat16 [8192, 4096], P('ctx', 'head'), may hold values from -6 to 6
- noise_mask: int32 [8192], P('ctx'), may hold values from 0 to 1, as said below
- block_order: int32 [32], replicated, may hold values from 0 to 31, as said below
Outputs:
- mixed: bfloat16 [8192, 4096], P('ctx', 'head')
- grad_q_noisy: bfloat16 [8192, 2048], P('ctx', 'head')
- grad_k_noisy: bfloat16 [8192, 2048], P('ctx', 'head')
- grad_v_noisy: bfloat16 [8192, 2048], P('ctx', 'head')
- grad_k_clean: bfloat16 [8192, 2048], P('ctx', 'head')
- grad_v_clean: bfloat16 [8192, 2048], P('ctx', 'head')
- grad_out_weight: float32 [2048, 4096], P('head', 'ctx')
Inputs may be any that keep to these rules, and one draw needn't show every extreme that they name: `noise_mask`: each block of 256 rows has its own share of ones. `block_order`: A permutation of the 32 block numbers; stored blocks 2j and 2j + 1 hold numbers that add up to 31.
All inputs are finite; a program needn't handle non-finite values.
Results may differ from a plain program's by a relative error of at most 0.04.
Values may be sent and summed in bfloat16 or wider, within the bound.
A program may use at most 128 MiB of HBM per device.

v0:
```python
import jax
import jax.numpy as jnp
from jax import lax
from jax.sharding import PartitionSpec as P

HEAD_DIM = 128
BLOCK = 256


big_negative = -1e30


def spread_blocks(block_ids):
    return jnp.broadcast_to(block_ids[:, None], (block_ids.shape[0], BLOCK)).reshape(-1)


def seen_mask(query_ids, key_ids, earlier):
    if earlier:
        return key_ids[None, :] < query_ids[:, None]
    return key_ids[None, :] == query_ids[:, None]


def masked_scores(queries, key_rows, visible, score_scale):
    raw_scores = (
        jnp.einsum("qhd,khd->hqk", queries, key_rows, preferred_element_type=jnp.float32)
        * score_scale
    )
    return jnp.where(visible[None], raw_scores, big_negative)


def absorb(state_tuple, queries, key_rows, value_rows, visible, score_scale):
    row_max, row_sum, weighted = state_tuple
    scores = masked_scores(queries, key_rows, visible, score_scale)
    new_max = jnp.maximum(row_max, jnp.max(scores, axis=2))
    weights = jnp.exp(scores - new_max[:, :, None])
    shrink = jnp.exp(row_max - new_max)
    row_sum = row_sum * shrink + jnp.sum(weights, axis=2)
    weighted = weighted * shrink[:, :, None] + jnp.einsum(
        "hqk,khd->hqd", weights.astype(jnp.bfloat16), value_rows, preferred_element_type=jnp.float32
    )
    return (new_max, row_sum, weighted)


def gradient_terms(
    queries, key_rows, value_rows, grad_rows, log_total, row_dot, visible, score_scale
):
    scores = masked_scores(queries, key_rows, visible, score_scale)
    probabilities = jnp.exp(scores - log_total[:, :, None])
    grad_probs = jnp.einsum(
        "qhd,khd->hqk", grad_rows, value_rows, preferred_element_type=jnp.float32
    )
    grad_scores = (probabilities * (grad_probs - row_dot[:, :, None])).astype(jnp.bfloat16)
    query_term = jnp.einsum(
        "hqk,khd->hqd", grad_scores, key_rows, preferred_element_type=jnp.float32
    )
    key_term = (
        jnp.einsum("hqk,qhd->khd", grad_scores, queries, preferred_element_type=jnp.float32)
        * score_scale
    )
    value_term = jnp.einsum(
        "hqk,qhd->khd",
        probabilities.astype(jnp.bfloat16),
        grad_rows,
        preferred_element_type=jnp.float32,
    )
    return (query_term, key_term, value_term)


def over_shards(step_rule, initial, gathered, tok_rows, shard_count):

    def one_turn(turn_index, state_tuple):
        first_row = turn_index * tok_rows
        block_piece = (
            lax.dynamic_slice_in_dim(gathered[0], first_row, tok_rows, 0),
            lax.dynamic_slice_in_dim(gathered[1], first_row, tok_rows, 0),
        )
        return step_rule(state_tuple, block_piece, first_row)

    return lax.fori_loop(0, shard_count, one_turn, initial)


def per_device(
    q_noisy, k_noisy, v_noisy, k_clean, v_clean, out_weight, cotangent, noise_mask, block_order
):
    tok_rows, feat_width = q_noisy.shape
    head_count = feat_width // HEAD_DIM
    shard_count = lax.axis_size("ctx")
    score_scale = HEAD_DIM ** (-0.5)
    block_count = tok_rows // BLOCK
    own_ids = spread_blocks(
        lax.dynamic_slice_in_dim(block_order, lax.axis_index("ctx") * block_count, block_count)
    )
    queries = q_noisy.reshape(tok_rows, head_count, HEAD_DIM)
    near_keys = k_noisy.reshape(tok_rows, head_count, HEAD_DIM)
    near_values = v_noisy.reshape(tok_rows, head_count, HEAD_DIM)
    loss_weight = noise_mask.astype(jnp.bfloat16)[:, None]
    same_block = seen_mask(own_ids, own_ids, False)

    def piece_ids(first_row, row_count):
        return spread_blocks(
            lax.dynamic_slice_in_dim(block_order, first_row // BLOCK, row_count // BLOCK)
        )

    empty_max = jnp.full((head_count, tok_rows), big_negative, jnp.float32)
    empty_sum = jnp.zeros((head_count, tok_rows), jnp.float32)
    empty_acc = jnp.zeros((head_count, tok_rows, HEAD_DIM), jnp.float32)
    start_state = absorb(
        (empty_max, empty_sum, empty_acc), queries, near_keys, near_values, same_block, score_scale
    )

    def attend(state_tuple, block_piece, first_row):
        key_rows = block_piece[0].reshape(-1, head_count, HEAD_DIM)
        value_rows = block_piece[1].reshape(-1, head_count, HEAD_DIM)
        visible = seen_mask(own_ids, piece_ids(first_row, key_rows.shape[0]), True)
        return absorb(state_tuple, queries, key_rows, value_rows, visible, score_scale)

    kept_pairs = (
        lax.all_gather(k_clean, "ctx", axis=0, tiled=True),
        lax.all_gather(v_clean, "ctx", axis=0, tiled=True),
    )
    row_max, row_sum, weighted = over_shards(attend, start_state, kept_pairs, tok_rows, shard_count)
    log_total = row_max + jnp.log(row_sum)
    attended_heads = weighted / row_sum[:, :, None]
    attended = (
        jnp.transpose(attended_heads, (1, 0, 2)).reshape(tok_rows, feat_width).astype(jnp.bfloat16)
    )
    out_term = jnp.dot(attended, out_weight, preferred_element_type=jnp.float32).astype(
        jnp.bfloat16
    )
    mixed = (
        lax.psum_scatter(out_term, "head", scatter_dimension=1, tiled=True)
        .astype(jnp.float32)
        .astype(jnp.bfloat16)
    )
    scaled_cot = lax.all_gather(cotangent, "head", axis=1, tiled=True) * loss_weight
    grad_sum = jnp.einsum("td,fd->tf", scaled_cot, out_weight, preferred_element_type=jnp.float32)
    weight_piece = jnp.einsum("tf,td->fd", attended, scaled_cot, preferred_element_type=jnp.float32)
    grad_sum, weight_grad = (grad_sum, weight_piece)
    grad_attended = grad_sum.astype(jnp.bfloat16)
    grad_out_weight = lax.psum_scatter(
        weight_grad.astype(jnp.bfloat16), "ctx", scatter_dimension=1, tiled=True
    ).astype(jnp.float32)
    grad_rows = grad_attended.reshape(tok_rows, head_count, HEAD_DIM)
    attended_rows = attended.reshape(tok_rows, head_count, HEAD_DIM)
    row_dot = jnp.transpose(
        jnp.sum(grad_rows.astype(jnp.float32) * attended_rows.astype(jnp.float32), axis=2)
    )
    query_near, key_near, value_near = gradient_terms(
        queries, near_keys, near_values, grad_rows, log_total, row_dot, same_block, score_scale
    )
    empty_grad = jnp.zeros((tok_rows * shard_count, feat_width), jnp.bfloat16)

    def back_step(state_tuple, block_piece, first_row):
        query_sum, key_grads, value_grads = state_tuple
        key_rows = block_piece[0].reshape(-1, head_count, HEAD_DIM)
        value_rows = block_piece[1].reshape(-1, head_count, HEAD_DIM)
        row_count = key_rows.shape[0]
        visible = seen_mask(own_ids, piece_ids(first_row, row_count), True)
        query_term, key_term, value_term = gradient_terms(
            queries, key_rows, value_rows, grad_rows, log_total, row_dot, visible, score_scale
        )
        key_grads = lax.dynamic_update_slice_in_dim(
            key_grads, key_term.reshape(row_count, feat_width).astype(jnp.bfloat16), first_row, 0
        )
        value_grads = lax.dynamic_update_slice_in_dim(
            value_grads,
            value_term.reshape(row_count, feat_width).astype(jnp.bfloat16),
            first_row,
            0,
        )
        return (query_sum + query_term, key_grads, value_grads)

    back_start = (query_near, empty_grad, empty_grad)
    query_sum, key_grads, value_grads = over_shards(
        back_step, back_start, kept_pairs, tok_rows, shard_count
    )
    clean_key_grad, clean_value_grad = (
        lax.psum_scatter(key_grads, "ctx", scatter_dimension=0, tiled=True).astype(jnp.float32),
        lax.psum_scatter(value_grads, "ctx", scatter_dimension=0, tiled=True).astype(jnp.float32),
    )
    grad_query = jnp.transpose(query_sum * score_scale, (1, 0, 2)).reshape(tok_rows, feat_width)
    return (
        mixed,
        grad_query.astype(jnp.bfloat16),
        key_near.reshape(tok_rows, feat_width).astype(jnp.bfloat16),
        value_near.reshape(tok_rows, feat_width).astype(jnp.bfloat16),
        clean_key_grad.astype(jnp.bfloat16),
        clean_value_grad.astype(jnp.bfloat16),
        grad_out_weight,
    )


def solution(mesh):
    in_specs = (
        P("ctx", "head"),
        P("ctx", "head"),
        P("ctx", "head"),
        P("ctx", "head"),
        P("ctx", "head"),
        P("head", None),
        P("ctx", "head"),
        P("ctx"),
        P(),
    )
    out_specs = (
        P("ctx", "head"),
        P("ctx", "head"),
        P("ctx", "head"),
        P("ctx", "head"),
        P("ctx", "head"),
        P("ctx", "head"),
        P("head", "ctx"),
    )
    return jax.shard_map(
        per_device, mesh=mesh, in_specs=in_specs, out_specs=out_specs, check_vma=False
    )
```

profile of v0, /device:TPU:1, one launch (start us, length us, event | category | flops | bytes accessed | tf_op | source)
XLA Modules:
  0.0 567.0 jit_solution(5287954185024907972)
XLA Ops:
  11.0 1.3 fusion.63
  12.8 62.7 %all-gather.4.cloned.1.call-done = bf16[8192,128]{1,0:T(8,128)(2,1)} async-done(((bf16[512,128]{1,0:T(8,128)(2,1)}), bf16[8192,128]{1,0:T(8,128)(2,1)}) %all-gather.4.cloned.1.call-update) | async-done | bytes 2097168 | tf_op jit(solution)/shard_map/all_gather | solution.py:118
  75.5 70.6 %all-gather.6.cloned.1.call-done = bf16[8192,128]{1,0:T(8,128)(2,1)} async-done(((bf16[512,128]{1,0:T(8,128)(2,1)}), bf16[8192,128]{1,0:T(8,128)(2,1)}) %all-gather.6.cloned.1.call-update) | async-done | bytes 2097168 | tf_op jit(solution)/shard_map/all_gather | solution.py:119
  146.1 48.7 %while.40 = (s32[]{:T(128)}, f32[1,512]{1,0:T(1,128)S(1)}, f32[1,512]{1,0:T(1,128)S(1)}, f32[1,512,128]{2,1,0:T(8,128)S(1)}, s32[32]{0:T(128)S(1)}, /*index=5*/b...) while((s32[]{:T(128)}, f32[1,512]{1,0:T(1,128)S(1)}, ...), condition=%wide.region_5.6_spmd.clone, body=%wide.region_2.5_spmd.clone.sunk | while | flops 136447008 | bytes 4112806 | solution.py:79
  147.8 1.3 fusion.102
  150.8 1.3 fusion.102
  153.9 1.3 fusion.102
  156.9 1.3 fusion.102
  160.0 1.3 fusion.102
  163.0 1.3 fusion.102
  166.0 1.3 fusion.102
  169.1 1.3 fusion.102
  172.1 1.3 fusion.102
  175.2 1.3 fusion.102
  178.2 1.3 fusion.102
  181.3 1.3 fusion.102
  184.3 1.3 fusion.102
  187.3 1.3 fusion.102
  190.4 1.3 fusion.102
  192.0 1.3 fusion.100
  193.5 1.3 fusion.102
  194.9 25.2 %all-gather.8.cloned.1.call-done = bf16[512,4096]{1,0:T(8,128)(2,1)} async-done(((bf16[512,256]{1,0:T(8,128)(2,1)}), bf16[512,4096]{1,0:T(8,128)(2,1)}) %all-gather.8.cloned.1.call-update) | async-done | bytes 4194320 | tf_op jit(solution)/shard_map/all_gather | solution.py:135
  220.2 3.9 multiply_reduce_fusion
  224.1 1.8 convolution_convert_fusion.2
  227.6 1.6 broadcast_in_dim.101.clone
  229.2 1.6 broadcast_in_dim.101
  230.8 94.7 %while.41 = (s32[]{:T(128)}, f32[1,512,128]{2,1,0:T(8,128)S(1)}, bf16[8192,128]{1,0:T(8,128)(2,1)}, bf16[8192,128]{1,0:T(8,128)(2,1)}, s32[32]{0:T(128)S(1)}, /*...) while((s32[]{:T(128)}, f32[1,512,128]{2,1,0:T(8,128)S(1)}, ...), condition=%wide.region_9.10_spmd.clone, body=%wide.region_8.9_spmd.clone.sunk | while | flops 337903648 | bytes 6443466 | solution.py:79
  231.1 1.3 fusion.113
  233.6 1.3 fusion.115
  237.0 1.3 fusion.113
  239.5 1.3 fusion.115
  242.9 1.3 fusion.113
  245.4 1.3 fusion.115
  248.8 1.3 fusion.113
  251.3 1.3 fusion.115
  254.7 1.3 fusion.113
  257.2 1.3 fusion.115
  260.6 1.3 fusion.113
  263.1 1.3 fusion.115
  266.6 1.3 fusion.113
  269.1 1.3 fusion.115
  272.5 1.3 fusion.113
  275.0 1.3 fusion.115
  278.4 1.3 fusion.113
  280.9 1.3 fusion.115
  284.3 1.3 fusion.113
  286.8 1.3 fusion.115
  290.2 1.3 fusion.113
  292.7 1.3 fusion.115
  296.2 1.3 fusion.113
  298.7 1.3 fusion.115
  302.1 1.3 fusion.113
  304.6 1.3 fusion.115
  308.0 1.3 fusion.113
  310.5 1.3 fusion.115
  313.9 1.3 fusion.113
  316.4 1.3 fusion.115
  319.8 1.3 fusion.113
  322.3 1.3 fusion.115
  326.2 3.3 convolution_convert_fusion.1
  332.2 1.5 convert_element_type.147
  333.7 53.2 %reduce-scatter.9.cloned.1.call-done = bf16[512,128]{1,0:T(8,128)(2,1)} async-done(((bf16[8192,128]{1,0:T(8,128)(2,1)}), bf16[512,128]{1,0:T(8,128)(2,1)}) %reduce-scatter.9.cloned.1.call-update) | async-done | bytes 131088 | tf_op jit(solution)/shard_map/reduce_scatter | solution.py:179
  387.0 73.5 %reduce-scatter.7.cloned.1.call-done = bf16[512,128]{1,0:T(8,128)(2,1)} async-done(((bf16[8192,128]{1,0:T(8,128)(2,1)}), bf16[512,128]{1,0:T(8,128)(2,1)}) %reduce-scatter.7.cloned.1.call-update) | async-done | bytes 131088 | tf_op jit(solution)/shard_map/reduce_scatter | solution.py:178
  460.4 99.7 %reduce-scatter.5.cloned.1.call-done = bf16[512,256]{1,0:T(8,128)(2,1)} async-done(((bf16[512,4096]{1,0:T(8,128)(2,1)}), bf16[512,256]{1,0:T(8,128)(2,1)}) %reduce-scatter.5.cloned.1.call-update) | async-done | bytes 262160 | tf_op jit(solution)/shard_map/reduce_scatter | solution.py:131
  (329 shorter events, 88.5 us)
Async XLA Ops:
  7.2 213.0 %copy-start = (bf16[128,4096]{1,0:T(8,128)(2,1)S(1)}, bf16[128,4096]{1,0:T(8,128)(2,1)}, u32[]{:S(2)}) copy-start(bf16[128,4096]{1,0:T(8,128)(2,1)} %param.18) | copy-start | bytes 3145732
  7.2 5.3 copy-start.2
  7.2 68.3 %all-gather.4.cloned.1.call-start = ((), (), s32[]{:S(2)}) async-start(), calls=%async_computation.4 | async-start | bytes 2228224 | tf_op jit(solution)/shard_map/all_gather | solution.py:118
  7.9 138.2 %all-gather.6.cloned.1.call-start = ((), (), s32[]{:S(2)}) async-start(), calls=%async_computation.5 | async-start | bytes 2228224 | tf_op jit(solution)/shard_map/all_gather | solution.py:119
  8.7 137.4 %copy-start.1 = (bf16[512,128]{1,0:T(8,128)(2,1)S(1)}, bf16[512,128]{1,0:T(8,128)(2,1)}, u32[]{:S(2)}) copy-start(bf16[512,128]{1,0:T(8,128)(2,1)} %param.13) | copy-start | bytes 393220
  8.7 137.4 %copy-start.4 = (s32[32]{0:T(128)S(1)}, s32[32]{0:T(128)}, u32[]{:S(2)}) copy-start(s32[32]{0:T(128)} %param.21) | copy-start | bytes 388
  8.7 211.5 %all-gather.8.cloned.1.call-start = ((), (), s32[]{:S(2)}) async-start(), calls=%async_computation.7 | async-start | bytes 4456448 | tf_op jit(solution)/shard_map/all_gather | solution.py:135
  9.4 322.8 %reduce-scatter.11.cloned.1.call-start = ((), (), s32[]{:S(2)}) async-start(), calls=%async_computation.10 | async-start | bytes 1114112 | tf_op jit(solution)/shard_map/reduce_scatter | solution.py:140
  220.2 3.9 copy-start.3
  225.9 161.0 %reduce-scatter.9.cloned.1.call-start = ((), (), s32[]{:S(2)}) async-start(), calls=%async_computation.9 | async-start | bytes 2228224 | tf_op jit(solution)/shard_map/reduce_scatter | solution.py:179
  325.6 134.9 %reduce-scatter.7.cloned.1.call-start = ((), (), s32[]{:S(2)}) async-start(), calls=%async_computation.8 | async-start | bytes 2228224 | tf_op jit(solution)/shard_map/reduce_scatter | solution.py:178
  326.1 234.0 %reduce-scatter.5.cloned.1.call-start = ((), (), s32[]{:S(2)}) async-start(), calls=%async_computation.6 | async-start | bytes 4456448 | tf_op jit(solution)/shard_map/reduce_scatter | solution.py:131
Sparse Core Ops, SparseCore 0:
  9.8 65.6 all-gather.3
  77.3 68.7 all-gather.5
  148.7 71.4 all-gather.7
  226.0 59.1 reduce-scatter.10
  325.7 61.2 reduce-scatter.8
  390.1 70.3 reduce-scatter.6
  466.0 94.1 reduce-scatter.4
where the time goes:
time: 569 us; the launch traced here: 567 us
  waiting for transfers between devices  388 us (68%)
  matrix products  144 us (25%)
  between operations  14.3 us (3%)
  local copies, waits for them, and re-layouts  12.4 us (2%)
  other arithmetic  6.62 us (1%)
    reduce_scatter x1, waiting for transfers between devices, per_device(): lax.psum_scatter(out_term, 'head', scatter_dimension=1, tiled=True)  99.7 us
    reduce_scatter x1, waiting for transfers between devices, per_device(): lax.psum_scatter(key_grads, 'ctx', scatter_dimension=0, tiled=True)  73.5 us
    all_gather x1, waiting for transfers between devices, per_device(): lax.all_gather(v_clean, 'ctx', axis=0, tiled=True)  70.6 us
    all_gather x1, waiting for transfers between devices, per_device(): lax.all_gather(k_clean, 'ctx', axis=0, tiled=True)  62.7 us
    reduce_scatter x1, waiting for transfers between devices, per_device(): lax.psum_scatter(value_grads, 'ctx', scatter_dimension=0, tiled=True)  53.2 us
    dot_general x33, matrix products, masked_scores(): jnp.einsum('qhd,khd->hqk', queries, key_rows, preferred_element_type=jnp....  41.4 us
    all_gather x1, waiting for transfers between devices, per_device(): lax.all_gather(cotangent, 'head', axis=1, tiled=True) * loss_weight  25.2 us
    dot_general x17, matrix products, gradient_terms(): jnp.einsum('hqk,khd->hqd', grad_scores, key_rows, preferred_element_type=...  21.6 us
  transfers between devices with their start and end apart: 7, of which 6 were waited for; matrix products, arithmetic and copies ran while one was open for 28% of the time, Pallas kernels for 0%

commit v1 on v0

v1 whole, which is shorter than its diff:
```python
import functools

import jax
import jax.numpy as jnp
from jax import lax
from jax.experimental import pallas as pl
from jax.experimental.pallas import tpu as pltpu
from jax.sharding import PartitionSpec as P

BLOCK = 256
HEAD_DIM = 128
SCALE = HEAD_DIM**-0.5
SCALE2 = SCALE * 1.4426950408889634
EMPTY = -1e30
NZ = 8
MESH = pl.DeviceIdType.MESH
BF = jnp.bfloat16
F32 = jnp.float32


def nt(a, b):
    return lax.dot_general(a, b, (((1,), (1,)), ((), ())), preferred_element_type=F32)


def nn(a, b):
    return lax.dot_general(a, b, (((1,), (0,)), ((), ())), preferred_element_type=F32)


def remote(src, dst, send_sem, recv_sem, device):
    return pltpu.make_async_remote_copy(
        src_ref=src,
        dst_ref=dst,
        send_sem=send_sem,
        recv_sem=recv_sem,
        device_id=device,
        device_id_type=MESH,
    )


def forward_tile(keys, values_t, queries, state):
    row_max, row_sum, acc = state
    scores = nt(keys, queries)
    new_max = jnp.maximum(row_max, jnp.max(scores, axis=0, keepdims=True))
    weights = jnp.exp2((scores - new_max) * SCALE2)
    shrink = jnp.exp2((row_max - new_max) * SCALE2)
    new_sum = row_sum * shrink + jnp.sum(weights, axis=0, keepdims=True)
    new_acc = acc * shrink + nn(values_t, weights.astype(BF))
    return new_max, new_sum, new_acc


def backward_tile(keys, values, keys_t, queries, grads, log_total, row_dot):
    probs = jnp.exp2(nt(keys, queries) * SCALE2 - log_total)
    grad_probs = nt(values, grads)
    grad_scores = (probs * (grad_probs - row_dot)).astype(BF)
    return nn(grad_scores, queries), nn(probs.astype(BF), grads), nn(keys_t, grad_scores)


def kernel(
    order, mask, q, kn, vn, kc, vc, w, cot,
    mixed, gq, gkn, gvn, gkc, gvc, gw,
    qs, kns, vns, kv, kt, vt, knt, vnt, ml, ml_in, acc, acc_out, acc_in,
    cotm, cot_all, w_cols, att_t, att_all, do_acc, dos, ld, dq, dq_out, dq_in,
    cb, rs_out, rs_in, gy_out, gy_in, g_out, g_in, stage,
    kv_ss, kv_rs, y_ss, y_rs, gy_ss, gy_rs, c_ss, c_rs, a_ss, a_rs, w_ss, w_rs,
    r_ss, r_rs, g_ss, g_rs,
):
    c = lax.axis_index("ctx")
    h = lax.axis_index("head")
    yl, z = c // NZ, c % NZ
    x, yh, co = h // 4, (h // 2) % 2, h % 2
    sends = []

    def go(copy):
        copy.start()
        sends.append(copy)

    def head_of(x_, yh_, co_):
        return x_ * 4 + yh_ * 2 + co_

    z_dev = [(yl * NZ + (z + 1) % NZ, h), (yl * NZ + (z + NZ - 1) % NZ, h)]
    y_ctx = (1 - yl) * NZ + z
    y_dev = (y_ctx, h)
    heads = [(h + k) % 16 for k in range(1, 16)]

    barrier = pltpu.get_barrier_semaphore()
    for dev in z_dev + [y_dev] + [(c, p) for p in heads]:
        pl.semaphore_signal(barrier, inc=1, device_id=dev, device_id_type=MESH)

    swap = order[2 * c] > order[2 * c + 1]

    def in_order(ref, i):
        first, second = ref[:BLOCK, :], ref[BLOCK:, :]
        return jnp.where(swap, first, second) if i else jnp.where(swap, second, first)

    def low_id(ctx):
        return jnp.minimum(order[2 * ctx], order[2 * ctx + 1])

    for i in range(2):
        kv[z, 0, i] = in_order(kc, i)
        kv[z, 1, i] = in_order(vc, i)
        qs[0, i] = in_order(q, i)
    row_id = lax.broadcasted_iota(jnp.int32, (128, 128), 0)
    col_id = lax.broadcasted_iota(jnp.int32, (128, 128), 1)
    for b in range(4):
        flags = jnp.broadcast_to(mask[b : b + 1, :].astype(F32), (128, 128))
        column = jnp.sum(jnp.where(row_id == col_id, flags, 0.0), axis=1, keepdims=True)
        rows = slice(b * 128, (b + 1) * 128)
        cotm[rows, :] = (cot[rows, :].astype(F32) * column).astype(BF)
    for i in range(2):
        cot_all[h, i * BLOCK : (i + 1) * BLOCK, :] = in_order(cotm, i)

    pl.semaphore_wait(barrier, 18)

    def kv_copy(d, s, t):
        slot = (z + NZ - (s - 1)) % NZ if d == 0 else (z + s - 1) % NZ
        return remote(
            kv.at[slot, t], kv.at[slot, t], kv_ss.at[d, s - 1, t], kv_rs.at[d, s - 1, t], z_dev[d]
        )

    def kv_wait(d, s, t):
        slot = (z + NZ - s) % NZ if d == 0 else (z + s) % NZ
        remote(
            kv.at[slot, t], kv.at[slot, t], kv_ss.at[d, s - 1, t], kv_rs.at[d, s - 1, t], z_dev[d]
        ).wait_recv()

    def head_copy(buf, ss, rs, index, slot, dev_head):
        return remote(buf.at[slot], buf.at[slot], ss.at[index], rs.at[index], (c, dev_head))

    yh_head = head_of(x, 1 - yh, co)
    sib = head_of(x, yh, 1 - co)

    def x_head(k, yh_, co_):
        return head_of((x + k) % 4, yh_, co_)

    def gather_begin(buf, ss, rs):
        go(head_copy(buf, ss, rs, 0, h, yh_head))
        for k in (1, 3, 2):
            go(head_copy(buf, ss, rs, k, h, x_head(k, yh, co)))
        go(head_copy(buf, ss, rs, 7, h, sib))

    def gather_second(buf, ss, rs):
        head_copy(buf, ss, rs, 0, yh_head, yh_head).wait_recv()
        for k in (1, 3, 2):
            go(head_copy(buf, ss, rs, 3 + k, yh_head, x_head(k, yh, co)))
        go(head_copy(buf, ss, rs, 8, yh_head, sib))

    def gather_pass(buf, ss, rs, second):
        for k in (1, 3, 2):
            index = 3 * second + k
            slot = head_of((x + 4 - k) % 4, 1 - yh if second else yh, co)
            head_copy(buf, ss, rs, index, slot, yh_head).wait_recv()
            go(head_copy(buf, ss, rs, 8 + index, slot, sib))

    def gather_end(buf, ss, rs):
        slots = [sib, head_of(x, 1 - yh, 1 - co)]
        slots += [head_of((x + 4 - k) % 4, yh, 1 - co) for k in (1, 2, 3)]
        slots += [head_of((x + 4 - k) % 4, 1 - yh, 1 - co) for k in (1, 2, 3)]
        for j, slot in enumerate(slots):
            head_copy(buf, ss, rs, 7 + j, slot, sib).wait_recv()

    def y_copy(index, src, dst):
        return remote(src, dst, y_ss.at[index], y_rs.at[index], y_dev)

    for t in range(2):
        for d in range(2):
            go(kv_copy(d, 1, t))
    q_copy = y_copy(0, qs.at[0], qs.at[1])
    go(q_copy)
    gather_begin(cot_all, c_ss, c_rs)

    for i in range(2):
        kns[i] = in_order(kn, i)
        vns[i] = in_order(vn, i)
        knt[i] = kns[i].T
        vnt[i] = vns[i].T

    def transpose_slot(slot):
        for i in range(2):
            kt[slot, i] = kv[slot, 0, i].T
            vt[slot, i] = kv[slot, 1, i].T

    def get_state(qd, i):
        return ml[qd, i], ml[qd, 2 + i], acc[qd, i]

    def put_state(qd, i, state):
        ml[qd, i], ml[qd, 2 + i] = (jnp.broadcast_to(v, (8, BLOCK)) for v in state[:2])
        acc[qd, i] = state[2]

    def rows_of(state):
        return state[0][:1], state[1][:1], state[2]

    def seen_high(qd, slot):
        q_ctx = (yl + qd * (1 - 2 * yl)) * NZ + z
        return low_id(yl * NZ + slot) > low_id(q_ctx)

    def forward_pair(qd, slot):
        high = seen_high(qd, slot)
        q_low, q_high = qs[qd, 0], qs[qd, 1]
        state_high = forward_tile(
            kv[slot, 0, 0], vt[slot, 0], q_high, rows_of(get_state(qd, 1))
        )
        state_low = rows_of(get_state(qd, 0))
        state = tuple(jnp.where(high, a, b) for a, b in zip(state_high, state_low))
        state = forward_tile(
            jnp.where(high, kv[slot, 0, 1], kv[slot, 0, 0]),
            jnp.where(high, vt[slot, 1], vt[slot, 0]),
            jnp.where(high, q_high, q_low),
            state,
        )
        put_state(qd, 0, tuple(jnp.where(high, b, a) for a, b in zip(state, state_low)))
        put_state(qd, 1, tuple(jnp.where(high, a, b) for a, b in zip(state, state_high)))

    empty = (
        jnp.full((1, BLOCK), EMPTY, F32),
        jnp.zeros((1, BLOCK), F32),
        jnp.zeros((HEAD_DIM, BLOCK), F32),
    )
    transpose_slot(z)
    for i in range(2):
        state = forward_tile(kns[i], vnt[i], qs[0, i], empty)
        if i == 1:
            state = forward_tile(kv[z, 0, 0], vt[z, 0], qs[0, 1], state)
        put_state(0, i, state)
        put_state(1, i, empty)
    q_copy.wait_recv()
    forward_pair(1, z)

    for s in range(1, 5):
        for t in range(2):
            for d in range(2):
                if s < 4 or t == d:
                    kv_wait(d, s, t)
                    if s < 3 or (s == 3 and t == d):
                        go(kv_copy(d, s + 1, t))
        if s < 4:

            def step(i, carry, s=s):
                slot = (z + NZ + (2 * i - 1) * s) % NZ
                transpose_slot(slot)
                forward_pair(0, slot)
                forward_pair(1, slot)
                return carry

            lax.fori_loop(0, 2, step, 0)
        else:
            slot = (z + 4) % NZ
            transpose_slot(slot)
            forward_pair(1, slot)
            for i in range(2):
                acc_out[i] = acc[1, i].astype(BF)
            ml_copy = y_copy(1, ml.at[1], ml_in)
            acc_copy = y_copy(2, acc_out, acc_in)
            go(ml_copy)
            go(acc_copy)
            forward_pair(0, slot)
        if s == 2:
            gather_second(cot_all, c_ss, c_rs)
        if s == 3:
            gather_pass(cot_all, c_ss, c_rs, 0)
    gather_pass(cot_all, c_ss, c_rs, 1)

    for k in range(1, 16):
        go(
            remote(
                w.at[:, pl.ds(pl.multiple_of(heads[k - 1] * 256, 256), 256)],
                w_cols.at[h],
                w_ss.at[k - 1],
                w_rs.at[k - 1],
                (c, heads[k - 1]),
            )
        )
    w_cols[h] = w[:, pl.ds(pl.multiple_of(h * 256, 256), 256)]

    gather_end(cot_all, c_ss, c_rs)
    do_acc[...] = jnp.zeros_like(do_acc)

    def add_piece(p, carry):
        columns = pl.ds(pl.multiple_of(p * 256, 256), 256)
        do_acc[...] += nt(cot_all[p], w[:, columns])
        return carry

    lax.fori_loop(0, 16, add_piece, 0)
    for i in range(2):
        dos[0, i] = do_acc[i * BLOCK : (i + 1) * BLOCK, :].astype(BF)
    do_copy = y_copy(3, dos.at[0], dos.at[1])
    go(do_copy)

    ml_copy.wait_recv()
    acc_copy.wait_recv()
    for i in range(2):
        own_max, own_sum, own_acc = rows_of(get_state(0, i))
        other_max, other_sum = ml_in[i][:1], ml_in[2 + i][:1]
        top = jnp.maximum(own_max, other_max)
        own_part = jnp.exp2((own_max - top) * SCALE2)
        other_part = jnp.exp2((other_max - top) * SCALE2)
        total = own_sum * own_part + other_sum * other_part
        weighted = own_acc * own_part + acc_in[i].astype(F32) * other_part
        attended_t = (weighted / total).astype(BF)
        att_t[:, i * BLOCK : (i + 1) * BLOCK] = attended_t
        att_all[h, i * BLOCK : (i + 1) * BLOCK, :] = attended_t.T
        grads_t = dos[0, i].T.astype(F32)
        row_dot = jnp.sum(grads_t * attended_t.astype(F32), axis=0, keepdims=True)
        ld[0, i] = jnp.broadcast_to(top * SCALE2 + jnp.log2(total), (8, BLOCK))
        ld[0, 2 + i] = jnp.broadcast_to(row_dot, (8, BLOCK))
    ld_copy = y_copy(4, ld.at[0], ld.at[1])
    go(ld_copy)
    gather_begin(att_all, a_ss, a_rs)

    def gy_slot(j):
        return (z + (4, 3, 5, 2, 6, 1, 7, 0)[j]) % NZ

    gy_copies = []
    for j in range(8):
        slot = gy_slot(j)
        gy_out[j] = nn(att_t[...], cot_all[(1 - yl) * NZ + slot]).astype(BF)
        gy_copies.append(remote(gy_out.at[j], gy_in.at[j], gy_ss.at[j], gy_rs.at[j], y_dev))
        go(gy_copies[-1])

    for i in range(2):
        key_term, value_term, query_term = backward_tile(
            kns[i], vns[i], knt[i], qs[0, i], dos[0, i], ld[0, i][:1], ld[0, 2 + i][:1]
        )
        stage[0, i] = (key_term * SCALE).astype(BF)
        stage[1, i] = value_term.astype(BF)
        dq[0, i] = query_term
        dq[1, i] = jnp.zeros_like(query_term)

    def unsort(index, out):
        for b in range(2):
            rows = jnp.where(swap, stage[index, 1 - b], stage[index, b])
            out[b * BLOCK : (b + 1) * BLOCK, :] = rows

    unsort(0, gkn)
    unsort(1, gvn)

    do_copy.wait_recv()
    ld_copy.wait_recv()

    def backward_pair(d, qd, slot, same):
        low, high = (
            backward_tile(
                kv[slot, 0, 0], kv[slot, 1, 0], kt[slot, 0],
                qs[qd, 1], dos[qd, 1], ld[qd, 1][:1], ld[qd, 3][:1],
            ),
            None,
        )
        if same:
            cb[d, 0, 0] = low[0]
            cb[d, 1, 0] = low[1]
            cb[d, 0, 1] = jnp.zeros_like(low[0])
            cb[d, 1, 1] = jnp.zeros_like(low[1])
            dq[qd, 1] += low[2]
            return
        pick = seen_high(qd, slot)

        def chosen(first, second):
            return jnp.where(pick, second, first)

        high = backward_tile(
            chosen(kv[slot, 0, 0], kv[slot, 0, 1]),
            chosen(kv[slot, 1, 0], kv[slot, 1, 1]),
            chosen(kt[slot, 0], kt[slot, 1]),
            chosen(qs[qd, 0], qs[qd, 1]),
            chosen(dos[qd, 0], dos[qd, 1]),
            chosen(ld[qd, 0][:1], ld[qd, 1][:1]),
            chosen(ld[qd, 2][:1], ld[qd, 3][:1]),
        )
        to_high = pick.astype(F32)
        to_low = 1.0 - to_high
        for t in range(2):
            new_low = low[t] + high[t] * to_low
            new_high = high[t] * to_high
            if qd == 0:
                cb[d, t, 0] = new_low
                cb[d, t, 1] = new_high
            else:
                cb[d, t, 0] += new_low
                cb[d, t, 1] += new_high
        dq[qd, 0] += high[2] * to_low
        dq[qd, 1] += low[2] + high[2] * to_high

    def contributions(s):
        if s in (0, 4):
            slot = (z + 4 - s) % NZ
            backward_pair(0, 0, slot, s == 4)
            backward_pair(0, 1, slot, False)
        else:

            def step(d, carry):
                slot = (z + NZ + (1 - 2 * d) * (4 - s)) % NZ
                backward_pair(d, 0, slot, False)
                backward_pair(d, 1, slot, False)
                return carry

            lax.fori_loop(0, 2, step, 0)

    factors = (SCALE, 1.0)

    def rs_copy(d, s, t):
        return remote(
            rs_out.at[d, s, t], rs_in.at[d, s, t], r_ss.at[d, s, t], r_rs.at[d, s, t], z_dev[d]
        )

    def g_copy(d, s):
        rows = pl.ds(64 * d, 64) if s == 0 else pl.ds(0, 128)
        return remote(
            g_out.at[d, s, rows], g_in.at[d, s, rows], g_ss.at[d, s], g_rs.at[d, s], z_dev[d]
        )

    def g_piece(j):
        gy_copies[j].wait_recv()
        own = nn(att_t[...], cot_all[yl * NZ + gy_slot(j)])
        return own + gy_in[j].astype(F32)

    contributions(0)
    for t in range(2):
        for i in range(2):
            rs_out[t, 0, t, i] = (cb[0, t, i] * factors[t]).astype(BF)
        go(rs_copy(t, 0, t))

    for s in range(1, 5):
        contributions(s)
        if s == 1:
            piece = g_piece(0).astype(BF)
            for d in range(2):
                g_out[d, 0] = piece
                go(g_copy(d, 0))
        else:
            for d in range(2):
                g_copy(d, s - 2).wait_recv()
                piece = g_piece(2 * (s - 1) - 1 + d)
                if s == 2:
                    half = slice(64 * d, 64 * d + 64)
                    rest = slice(64 - 64 * d, 128 - 64 * d)
                    g_out[d, 1, half] = (piece[half] + g_in[d, 0, half].astype(F32)).astype(BF)
                    g_out[d, 1, rest] = piece[rest].astype(BF)
                else:
                    g_out[d, s - 1] = (piece + g_in[d, s - 2].astype(F32)).astype(BF)
                go(g_copy(d, s - 1))
        if s < 4:
            for t in range(2):
                for d in range(2):
                    if s == 1 and t != d:
                        for i in range(2):
                            rs_out[d, 1, t, i] = (cb[d, t, i] * factors[t]).astype(BF)
                    else:
                        rs_copy(d, s - 1, t).wait_recv()
                        for i in range(2):
                            rs_out[d, s, t, i] = (
                                cb[d, t, i] * factors[t] + rs_in[d, s - 1, t, i].astype(F32)
                            ).astype(BF)
                    go(rs_copy(d, s, t))
        if s == 1:
            gather_second(att_all, a_ss, a_rs)
        if s == 2:
            gather_pass(att_all, a_ss, a_rs, 0)
        if s == 3:
            gather_pass(att_all, a_ss, a_rs, 1)

    for i in range(2):
        dq_out[i] = (dq[1, i] * SCALE).astype(BF)
    dq_copy = y_copy(5, dq_out, dq_in)
    go(dq_copy)

    gather_end(att_all, a_ss, a_rs)
    for k in range(1, 16):
        source = (h + 16 - k) % 16
        remote(
            w.at[:, pl.ds(0, 256)], w_cols.at[source], w_ss.at[k - 1], w_rs.at[k - 1], (c, source)
        ).wait_recv()
    total = nn(att_all[0], w_cols[0])
    for p in range(1, 16):
        total = total + nn(att_all[p], w_cols[p])
    cotm[...] = total.astype(BF)
    for b in range(2):
        mixed[b * BLOCK : (b + 1) * BLOCK, :] = in_order(cotm, b)

    dq_copy.wait_recv()
    for i in range(2):
        stage[2, i] = (dq[0, i] * SCALE + dq_in[i].astype(F32)).T.astype(BF)
    unsort(2, gq)

    piece = g_piece(7)
    for d in range(2):
        g_copy(d, 3).wait_recv()
        piece = piece + g_in[d, 3].astype(F32)
    gw[...] = piece

    for t in range(2):
        for d in range(2):
            rs_copy(d, 3, t).wait_recv()
        for i in range(2):
            stage[3 + t, i] = (
                cb[0, t, i] * factors[t]
                + rs_in[0, 3, t, i].astype(F32)
                + rs_in[1, 3, t, i].astype(F32)
            ).astype(BF)
    unsort(3, gkc)
    unsort(4, gvc)

    for copy in sends:
        copy.wait_send()


def per_device(q, kn, vn, kc, vc, w, cot, noise_mask, block_order):
    vmem = pl.BlockSpec(memory_space=pltpu.VMEM)
    smem = pl.BlockSpec(memory_space=pltpu.SMEM)
    rows, width = q.shape
    blk = (BLOCK, HEAD_DIM)
    tblk = (HEAD_DIM, BLOCK)
    dma = pltpu.SemaphoreType.DMA
    narrow = jax.ShapeDtypeStruct((rows, width), BF)
    scratch = [
        pltpu.VMEM((2, 2) + blk, BF),
        pltpu.VMEM((2,) + blk, BF),
        pltpu.VMEM((2,) + blk, BF),
        pltpu.VMEM((NZ, 2, 2) + blk, BF),
        pltpu.VMEM((NZ, 2) + tblk, BF),
        pltpu.VMEM((NZ, 2) + tblk, BF),
        pltpu.VMEM((2,) + tblk, BF),
        pltpu.VMEM((2,) + tblk, BF),
        pltpu.VMEM((2, 4, 8, BLOCK), F32),
        pltpu.VMEM((4, 8, BLOCK), F32),
        pltpu.VMEM((2, 2) + tblk, F32),
        pltpu.VMEM((2,) + tblk, BF),
        pltpu.VMEM((2,) + tblk, BF),
        pltpu.VMEM((rows, 256), BF),
        pltpu.VMEM((16, rows, 256), BF),
        pltpu.VMEM((16, HEAD_DIM, 256), BF),
        pltpu.VMEM((HEAD_DIM, rows), BF),
        pltpu.VMEM((16, rows, HEAD_DIM), BF),
        pltpu.VMEM((rows, HEAD_DIM), F32),
        pltpu.VMEM((2, 2) + blk, BF),
        pltpu.VMEM((2, 4, 8, BLOCK), F32),
        pltpu.VMEM((2, 2) + tblk, F32),
        pltpu.VMEM((2,) + tblk, BF),
        pltpu.VMEM((2,) + tblk, BF),
        pltpu.VMEM((2, 2, 2) + blk, F32),
        pltpu.VMEM((2, 4, 2, 2) + blk, BF),
        pltpu.VMEM((2, 4, 2, 2) + blk, BF),
        pltpu.VMEM((8, HEAD_DIM, 256), BF),
        pltpu.VMEM((8, HEAD_DIM, 256), BF),
        pltpu.VMEM((2, 4, HEAD_DIM, 256), BF),
        pltpu.VMEM((2, 4, HEAD_DIM, 256), BF),
        pltpu.VMEM((5, 2) + blk, BF),
        dma((2, 4, 2)), dma((2, 4, 2)),
        dma((6,)), dma((6,)),
        dma((8,)), dma((8,)),
        dma((15,)), dma((15,)),
        dma((15,)), dma((15,)),
        dma((15,)), dma((15,)),
        dma((2, 4, 2)), dma((2, 4, 2)),
        dma((2, 4)), dma((2, 4)),
    ]
    return pl.pallas_call(
        kernel,
        out_shape=(
            jax.ShapeDtypeStruct(cot.shape, BF),
            narrow, narrow, narrow, narrow, narrow,
            jax.ShapeDtypeStruct((HEAD_DIM, 256), F32),
        ),
        in_specs=[smem] + [vmem] * 8,
        out_specs=(vmem,) * 7,
        scratch_shapes=scratch,
        compiler_params=pltpu.CompilerParams(
            collective_id=0, has_side_effects=True, vmem_limit_bytes=56 * 2**20
        ),
        name="block_attention",
    )(block_order, noise_mask.reshape(4, 128), q, kn, vn, kc, vc, w, cot)


def solution(mesh):
    spread = P("ctx", "head")
    return jax.shard_map(
        per_device,
        mesh=mesh,
        in_specs=(spread,) * 5 + (P("head", None), spread, P("ctx"), P()),
        out_specs=(spread,) * 6 + (P("head", "ctx"),),
        check_vma=False,
    )
```

time: 569 us -> 97.2 us (0.17)
  waiting for transfers between devices: 388 us -> 0 us
  matrix products: 144 us -> 0 us
  Pallas kernels: 0 us -> 87.8 us
  between operations: 14.3 us -> 0.66 us
  other arithmetic: 6.62 us -> 0 us
    reduce_scatter x4 -> x0, waiting for transfers between devices: 226 us -> none  [the longest x1 99.7 us: per_device(): lax.psum_scatter(out_term, 'head', scatter_dimension=1, tiled=True)]
    all_gather x3 -> x0, waiting for transfers between devices: 158 us -> none  [the longest x1 70.6 us: per_device(): lax.all_gather(v_clean, 'ctx', axis=0, tiled=True)]
    dot_general x121 -> x0, matrix products: 144 us -> none  [the longest x33 41.4 us: masked_scores(): jnp.einsum('qhd,khd->hqk', queries, key_rows, preferred_element_type=jnp....]
    pallas_call x0 -> x1, Pallas kernels: none -> 87.8 us  [per_device(): pl.pallas_call(kernel, out_shape=(jax.ShapeDtypeStruct(cot.shape, BF), na...]
    unnamed x14 -> x19, local copies, waits for them, and re-layouts: 0.99 us -> 7.11 us
  transfers between devices with their start and end apart: 7 -> 0, of which waited for: 6 -> 0; matrix products, arithmetic and copies ran while one was open for 28% -> 0% of each run, Pallas kernels for 0% -> 0%
where the time goes in v1:
time: 97.2 us; the launch traced here: 95.6 us
  Pallas kernels  87.8 us (90%)
  local copies, waits for them, and re-layouts  7.11 us (7%)
    pallas_call x1, Pallas kernels, per_device(): pl.pallas_call(kernel, out_shape=(jax.ShapeDtypeStruct(cot.shape, BF), na...  87.8 us
    unnamed x19, local copies, waits for them, and re-layouts  7.11 us

profile of v1, /device:TPU:1, one launch (start us, length us, event | category | flops | bytes accessed | tf_op | source)
XLA Modules:
  0.0 95.6 jit_solution(15074899501072759798)
XLA Ops:
  0.6 87.8 %block_attention.1 = (bf16[512,256]{1,0:T(8,128)(2,1)}, bf16[512,128]{1,0:T(8,128)(2,1)}, bf16[512,128]{1,0:T(8,128)(2,1)}, bf16[512,128]{1,0:T(8,128)(2,1)}, bf...) custom-call(s32[32]{0:T(128)} %order.1, s32[4,128]{1,0:T(4,128)} %bitcast.1, ...), custom_call_target="tpu_custom_call" | custom-call | tf_op jit(solution)/shard_map/block_attention/pallas_call | solution.py:555
  88.5 0.0 copy-start.5
  88.5 1.7 %copy.23 = bf16[512,256]{1,0:T(8,128)(2,1)} copy(bf16[512,256]{1,0:T(8,128)(2,1)} %get-tuple-element.14) | data formatting | bytes 524288
  90.2 0.0 copy-done.5
  90.2 0.0 copy-start.4
  90.2 0.7 copy.24
  90.9 0.3 copy-done.4
  91.2 0.0 copy-start.3
  91.2 0.7 copy.25
  91.8 0.3 copy-done.3
  92.1 0.0 copy-start.2
  92.1 0.7 copy.26
  92.8 0.3 copy-done.2
  93.1 0.0 copy-start.1
  93.1 0.7 copy.27
  93.7 0.3 copy-done.1
  94.0 0.0 copy-start
  94.0 0.7 copy.28
  94.7 0.3 copy-done
  95.0 0.7 copy.29
Async XLA Ops:
  88.5 1.7 %copy-start.5 = (bf16[512,128]{1,0:T(8,128)(2,1)S(1)}, bf16[512,128]{1,0:T(8,128)(2,1)}, u32[]{:S(2)}) copy-start(bf16[512,128]{1,0:T(8,128)(2,1)} %get-tuple-element.15) | copy-start | bytes 393220
  90.2 1.0 copy-start.4
  91.2 1.0 copy-start.3
  92.1 1.0 copy-start.2
  93.1 1.0 copy-start.1
  94.0 1.0 copy-start
